TPU v7x, 32 devices: a whole 2x2x4 slice. The times are simulated.
32 devices in a mesh: row: 8 (over y, x, core), col: 4 (over z).
Axes of the slice: x: 2, y: 2, z: 4, core: 2. Of those that a mesh axis runs over, the one named last changes fastest.
Arguments:
- trail_adjoint: float32 [4, 8, 128, 8, 4, 128], P(None, 'row', None, None, 'col'), may hold values from -24 to 24, as said below
- factor_panels: float32 [4, 8, 128, 2, 128], P(None, 'row'), may hold values from -1 to 2, as said below
- factor_adjoint: float32 [4, 8, 128, 2, 128], P(None, 'row'), may hold values from -6 to 6
- diag_inverse: float32 [2, 128, 128], replicated, may hold values from -1 to 1, as said below
Outputs:
- cov_adjoint: float32 [4, 8, 128, 8, 4, 128], P(None, 'row', None, None, 'col')
Inputs may be any that keep to these rules, and one draw needn't show every extreme that they name: trail_adjoint read as the matrix H is symmetric. `factor_panels`: read as Lp, panel k is zero on rows before k * 128, and its rows D_k form a lower triangular block with diagonal entries from 1 to 2. diag_inverse[k] is the inverse of the lower triangular block of panel k on the rows D_k.
All inputs are finite; a program needn't handle non-finite values.
Results may differ from a plain program's by a relative error of at most 0.0002.
Values sent between devices are 32-bit elements; how exact they have to be, the bound alone decides.
A program may use at most 64 MiB of HBM per device.

v0:
```python
import jax
import jax.numpy as jnp
from jax import lax
from jax.sharding import PartitionSpec as P


def product(left_matrix, right_matrix):
    return jnp.dot(
        left_matrix,
        right_matrix,
        precision=lax.Precision.HIGHEST,
        preferred_element_type=jnp.float32,
    )


def halved_lower(matrix):
    return jnp.tril(matrix) - 0.5 * matrix * jnp.eye(matrix.shape[0], dtype=matrix.dtype)


def diagonal_adjoint(lower_block, given_block, gram_block, inverse):
    reduced = jnp.tril(given_block - gram_block)
    inner_block = halved_lower(product(lower_block.T, reduced))
    mixed_block = product(product(inverse.T, inner_block), inverse)
    return 0.5 * (mixed_block + mixed_block.T)


def to_columns(values, tile_size):
    column_index = lax.axis_index("col")
    col_count = lax.axis_size("col")
    row_count = lax.axis_size("row")
    local_tiles = values.shape[0] // tile_size
    breadth = values.shape[1]
    everything = lax.all_gather(
        values.reshape(local_tiles, 1, tile_size, breadth), "row", axis=1, tiled=True
    )
    arranged = everything.reshape(
        local_tiles * row_count // col_count, col_count, tile_size, breadth
    )
    picked = lax.dynamic_index_in_dim(arranged, column_index, 1, keepdims=False)
    result_cols = picked.reshape(-1, breadth)
    return result_cols


def row_total(values):
    return lax.psum(values, "col")


def column_total(values):
    return lax.psum(values, "row")


def per_device(trail_adjoint, factor_panels, factor_adjoint, diag_inverse):
    tile_rows = trail_adjoint.shape[0]
    tile_size = trail_adjoint.shape[2]
    tile_cols = trail_adjoint.shape[3]
    row_index = lax.axis_index("row")
    column_index = lax.axis_index("col")
    row_count = lax.axis_size("row")
    matrix = trail_adjoint.reshape(tile_rows * tile_size, tile_cols * tile_size)
    lower_panels = factor_panels.reshape(tile_rows * tile_size, 2 * tile_size)
    given_panels = factor_adjoint.reshape(tile_rows * tile_size, 2 * tile_size)
    local_rows = jnp.arange(tile_rows * tile_size, dtype=jnp.int32)
    global_rows = (
        local_rows // tile_size * row_count + row_index
    ) * tile_size + local_rows % tile_size
    for panel_index in (1, 0):
        masked_start_col = panel_index * tile_size
        masked_below_mask = (global_rows >= masked_start_col + tile_size)[:, None]
        lower_cols = jnp.where(
            masked_below_mask, lower_panels[:, masked_start_col : masked_start_col + tile_size], 0.0
        )
        remote = to_columns(lower_cols, tile_size)
        products = row_total(product(matrix, remote))
        adjoint_start_col = panel_index * tile_size
        below_mask = (global_rows >= adjoint_start_col + tile_size)[:, None]
        adjoint_cols = jnp.where(
            below_mask,
            given_panels[:, adjoint_start_col : adjoint_start_col + tile_size] - 2.0 * products,
            0.0,
        )
        scaled = product(adjoint_cols, diag_inverse[panel_index])
        (gram_block,) = column_total((product(scaled.T, lower_cols),))
        start_col = panel_index * tile_size
        stop_col = start_col + tile_size
        diag_update = diagonal_adjoint(
            lower_panels[:tile_size, start_col:stop_col],
            given_panels[:tile_size, start_col:stop_col],
            gram_block,
            diag_inverse[panel_index],
        )
        scaled_cols = to_columns(scaled, tile_size)
        current = matrix
        owner_column = column_index == panel_index
        owner_row = row_index == panel_index
        current = current.at[:, :tile_size].add(jnp.where(owner_column, 0.5 * scaled, 0.0))
        current = current.at[:tile_size, :].add(jnp.where(owner_row, 0.5 * scaled_cols.T, 0.0))
        current = current.at[:tile_size, :tile_size].add(
            jnp.where(owner_row & owner_column, diag_update, 0.0)
        )
        matrix = current
    return matrix.reshape(trail_adjoint.shape)


def solution(mesh):
    placed = (
        P(None, "row", None, None, "col", None),
        P(None, "row", None, None, None),
        P(None, "row", None, None, None),
        P(),
    )
    return jax.shard_map(
        per_device,
        mesh=mesh,
        in_specs=placed,
        out_specs=P(None, "row", None, None, "col", None),
        check_vma=False,
    )
```

profile of v0, /device:TPU:0, one launch (start us, length us, event | category | flops | bytes accessed | tf_op | source)
XLA Modules:
  0.0 332.5 jit_solution(12712488365732746142)
XLA Ops:
  6.6 1.2 copy.34
  7.8 1.0 slice_select_fusion
  8.8 31.0 %all-gather.5.cloned.1.call-done = f32[4,8,128,128]{3,2,1,0:T(8,128)} async-done(((f32[4,1,128,128]{3,2,1,0:T(8,128)}), f32[4,8,128,128]{3,2,1,0:T(8,128)}) %all-gather.5.cloned.1.call-update) | async-done | bytes 2097168 | tf_op jit(solution)/shard_map/all_gather | solution.py:33
  39.9 1.1 constant_dynamic-slice_fusion.1
  41.0 2.5 convolution_bitcast_fusion
  43.6 0.7 all-gather.9.cloned.1.call-update
  44.3 2.1 copy.33
  46.4 1.1 copy.35
  47.5 0.6 compare_reduce_fusion
  48.2 30.8 %all-reduce.5.cloned.1.call-done = f32[512,128]{1,0:T(8,128)} async-done(((f32[512,128]{1,0:T(8,128)}), f32[512,128]{1,0:T(8,128)}) %all-reduce.5.cloned.1.call-update) | async-done | bytes 262160 | tf_op jit(solution)/shard_map/psum | solution.py:45
  79.0 2.0 fusion
  81.0 0.7 copy-done.3
  81.7 1.2 fusion.79
  83.6 25.1 %all-gather.9.cloned.1.call-done = f32[4,8,128,128]{3,2,1,0:T(8,128)} async-done(((f32[4,1,128,128]{3,2,1,0:T(8,128)}), f32[4,8,128,128]{3,2,1,0:T(8,128)}) %all-gather.9.cloned.1.call-update) | async-done | bytes 2097168 | tf_op jit(solution)/shard_map/all_gather | solution.py:33
  108.7 1.9 constant_dynamic-slice_fusion
  110.6 53.8 %all-reduce.7.cloned.1.call-done = f32[128,128]{1,0:T(8,128)} async-done(((f32[128,128]{1,0:T(8,128)}), f32[128,128]{1,0:T(8,128)}) %all-reduce.7.cloned.1.call-update) | async-done | bytes 65552 | tf_op jit(solution)/shard_map/psum | solution.py:49
  164.4 1.1 convolution_bitcast_fusion.2
  166.2 27.3 %all-gather.7.cloned.1.call-done = f32[4,8,128,128]{3,2,1,0:T(8,128)} async-done(((f32[4,1,128,128]{3,2,1,0:T(8,128)}), f32[4,8,128,128]{3,2,1,0:T(8,128)}) %all-gather.7.cloned.1.call-update) | async-done | bytes 2097168 | tf_op jit(solution)/shard_map/all_gather | solution.py:33
  193.5 1.9 multiply_select_fusion.1
  195.4 2.0 copy.23
  197.4 1.3 constant_dynamic-update-slice_fusion.1
  198.8 2.5 fusion.80
  201.3 35.4 %all-reduce.9.cloned.1.call-done = f32[512,128]{1,0:T(8,128)} async-done(((f32[512,128]{1,0:T(8,128)}), f32[512,128]{1,0:T(8,128)}) %all-reduce.9.cloned.1.call-update) | async-done | bytes 262160 | tf_op jit(solution)/shard_map/psum | solution.py:45
  236.8 2.0 fusion.1
  238.8 0.7 copy-done.4
  239.5 1.2 fusion.81
  240.8 0.7 all-gather.11.cloned.1.call-update
  241.5 51.6 %all-reduce.11.cloned.1.call-done = f32[128,128]{1,0:T(8,128)} async-done(((f32[128,128]{1,0:T(8,128)}), f32[128,128]{1,0:T(8,128)}) %all-reduce.11.cloned.1.call-update) | async-done | bytes 65552 | tf_op jit(solution)/shard_map/psum | solution.py:49
  293.1 1.1 convolution_bitcast_fusion.1
  294.9 27.4 %all-gather.11.cloned.1.call-done = f32[4,8,128,128]{3,2,1,0:T(8,128)} async-done(((f32[4,1,128,128]{3,2,1,0:T(8,128)}), f32[4,8,128,128]{3,2,1,0:T(8,128)}) %all-gather.11.cloned.1.call-update) | async-done | bytes 2097168 | tf_op jit(solution)/shard_map/all_gather | solution.py:33
  322.3 1.1 multiply_select_fusion
  323.9 1.8 copy.28
  (37 shorter events, 2.7 us)
Async XLA Ops:
  6.5 34.4 %copy-start = (f32[4,1,128,8,1,128]{5,4,3,2,1,0:T(1,128)S(1)}, f32[4,1,128,8,1,128]{5,4,3,2,1,0:T(1,128)}, u32[]{:S(2)}) copy-start(f32[4,1,128,8,1,128]{5,4,3,2,1,0:T(1,128)} %param.16) | copy-start | bytes 6291460
  6.5 33.4 %all-gather.5.cloned.1.call-start = ((), (), s32[]{:S(2)}) async-start(), calls=%async_computation | async-start | bytes 2359296 | tf_op jit(solution)/shard_map/all_gather | solution.py:33
  8.8 70.2 %all-reduce.5.cloned.1.call-start = ((), (), s32[]{:S(2)}) async-start(), calls=%async_computation.1 | async-start | bytes 524288 | tf_op jit(solution)/shard_map/psum | solution.py:45
  43.5 65.2 %all-gather.9.cloned.1.call-start = ((), (), s32[]{:S(2)}) async-start(), calls=%async_computation.4 | async-start | bytes 2359296 | tf_op jit(solution)/shard_map/all_gather | solution.py:33
  44.2 34.7 %copy-start.6 = (f32[2,128,128]{2,1,0:T(8,128)S(1)}, f32[2,128,128]{2,1,0:T(8,128)}, u32[]{:S(2)}) copy-start(f32[2,128,128]{2,1,0:T(8,128)} %param.19) | copy-start | bytes 393220
  44.3 120.1 %all-reduce.7.cloned.1.call-start = ((), (), s32[]{:S(2)}) async-start(), calls=%async_computation.3 | async-start | bytes 131072 | tf_op jit(solution)/shard_map/psum | solution.py:49
  46.4 35.3 %copy-start.2 = (f32[512,128]{1,0:T(8,128)S(1)}, f32[512,128]{1,0:T(8,128)}, u32[]{:S(2)}) copy-start(f32[512,128]{1,0:T(8,128)} %get-tuple-element.82) | copy-start | bytes 786436
  81.0 0.7 copy-start.3
  83.0 110.5 %all-gather.7.cloned.1.call-start = ((), (), s32[]{:S(2)}) async-start(), calls=%async_computation.2 | async-start | bytes 2359296 | tf_op jit(solution)/shard_map/all_gather | solution.py:33
  83.6 153.2 %all-reduce.9.cloned.1.call-start = ((), (), s32[]{:S(2)}) async-start(), calls=%async_computation.5 | async-start | bytes 524288 | tf_op jit(solution)/shard_map/psum | solution.py:45
  197.4 1.3 copy-start.5
  198.8 40.7 %copy-start.1 = (f32[512,128]{1,0:T(8,128)S(1)}, f32[512,128]{1,0:T(8,128)}, u32[]{:S(2)}) copy-start(f32[512,128]{1,0:T(8,128)} %get-tuple-element.81) | copy-start | bytes 786436
  201.3 91.8 %all-reduce.11.cloned.1.call-start = ((), (), s32[]{:S(2)}) async-start(), calls=%async_computation.7 | async-start | bytes 131072 | tf_op jit(solution)/shard_map/psum | solution.py:49
  238.8 0.7 copy-start.4
  240.7 81.6 %all-gather.11.cloned.1.call-start = ((), (), s32[]{:S(2)}) async-start(), calls=%async_computation.6 | async-start | bytes 2359296 | tf_op jit(solution)/shard_map/all_gather | solution.py:33
Sparse Core Ops, SparseCore 0:
  9.3 30.5 all-gather.4
  43.6 35.2 all-reduce.4
  81.0 27.6 all-gather.8
  111.9 52.4 all-reduce.6
  166.1 27.2 all-gather.6
  201.4 35.2 all-reduce.8
  240.9 52.2 all-reduce.10
  295.0 27.2 all-gather.10
where the time goes:
time: 333 us; the launch traced here: 332 us
  waiting for transfers between devices  284 us (85%)
  matrix products  14.9 us (4%)
  between operations  13.7 us (4%)
  local copies, waits for them, and re-layouts  13 us (4%)
  other arithmetic  6.17 us (2%)
    all_gather x4, waiting for transfers between devices, to_columns(): lax.all_gather(values.reshape(local_tiles, 1, tile_size, breadth), 'row',...  111 us
    psum x2, waiting for transfers between devices, column_total(): return lax.psum(values, 'row')  105 us
    psum x2, waiting for transfers between devices, row_total(): return lax.psum(values, 'col')  66.2 us
    dot_general x12, matrix products, product(): jnp.dot(left_matrix, right_matrix, precision=lax.Precision.HIGHEST, prefe...  14.9 us
    unnamed x18, local copies, waits for them, and re-layouts  7.64 us
  transfers between devices with their start and end apart: 8, of which 8 were waited for; matrix products, arithmetic and copies ran while one was open for 4% of the time, Pallas kernels for 0%

commit v1 on v0

v1 whole, which is shorter than its diff:
```python
import functools

import jax
import jax.numpy as jnp
from jax import lax
from jax.experimental import pallas as pl
from jax.experimental.pallas import tpu as pltpu
from jax.sharding import PartitionSpec as P

MESH = pl.DeviceIdType.MESH


def dot(a, b, ca=1, cb=0):
    return lax.dot_general(
        a,
        b,
        (((ca,), (cb,)), ((), ())),
        precision=lax.Precision.HIGHEST,
        preferred_element_type=jnp.float32,
    )


def halved_lower(matrix):
    rows = lax.broadcasted_iota(jnp.int32, matrix.shape, 0)
    cols = lax.broadcasted_iota(jnp.int32, matrix.shape, 1)
    return jnp.where(rows > cols, matrix, jnp.where(rows == cols, 0.5 * matrix, 0.0))


def lower(matrix):
    rows = lax.broadcasted_iota(jnp.int32, matrix.shape, 0)
    cols = lax.broadcasted_iota(jnp.int32, matrix.shape, 1)
    return jnp.where(rows >= cols, matrix, 0.0)


def diagonal_adjoint(lower_block, given_block, gram_block, inverse):
    inner = halved_lower(dot(lower_block, lower(given_block - gram_block), 0, 0))
    mixed = dot(dot(inverse, inner, 0, 0), inverse)
    return 0.5 * (mixed + mixed.T)


def kernel(
    sizes,
    h_ref,
    lp_ref,
    lb_ref,
    inv_ref,
    out_ref,
    pan,
    raw,
    raw1,
    l10,
    cb,
    pbuf,
    recv,
    gpart,
    grecv,
    gred,
    g2,
    gsum,
    g3,
    ybuf,
    rowupd,
    colupd,
    cb_send,
    cb_recv,
    l_send,
    l_recv,
    raw_sem,
    p_send,
    p_recv,
    ga_send,
    ga_recv,
    gb_send,
    gb_recv,
    gc_send,
    gc_recv,
    y_send,
    row_recv,
    col_recv,
):
    n_row, n_col, R, T, nb = sizes
    s = n_row // T
    piece = 3 * nb // T
    r = lax.axis_index("row")
    c = lax.axis_index("col")
    wk = r // s
    is_worker = lax.rem(r, s) == 0
    tile = wk * n_col + c
    dst_row = lax.rem(tile, n_row)
    dst_slot = tile // n_row

    def remote(src, dst, send, receive, row, col):
        return pltpu.make_async_remote_copy(
            src_ref=src,
            dst_ref=dst,
            send_sem=send,
            recv_sem=receive,
            device_id=(row, col),
            device_id_type=MESH,
        )

    def slot_source(i):
        g = i * n_row + r
        return lax.rem(g, n_col), (g // n_col) * s

    barrier = pltpu.get_barrier_semaphore()
    for d in range(1, n_row):
        pl.semaphore_signal(
            barrier, inc=1, device_id=(lax.rem(r + d, n_row), c), device_id_type=MESH
        )
    for k in range(2):
        for i in range(R):
            src_col, src_row = slot_source(i)

            @pl.when((c == k) & (src_col != k))
            def _():
                pl.semaphore_signal(
                    barrier, inc=1, device_id=(src_row, src_col), device_id_type=MESH
                )

        for other in range(n_col):
            if other != k:

                @pl.when((c == k) & is_worker)
                def _():
                    pl.semaphore_signal(
                        barrier, inc=1, device_id=(r, other), device_id_type=MESH
                    )

    for i in range(R):
        for k in range(2):
            keep = (i * n_row + r > k) if i == 0 else True
            at = pl.ds(i * nb * 2 + k, nb, stride=2)
            lv, bv = lp_ref[at, :], lb_ref[at, :]
            if i == 0:
                lv = jnp.where(keep, lv, 0.0)
                bv = jnp.where(keep, bv, 0.0)
            pan[i, k] = lv
            pan[i, 2 + k] = bv
    for k in range(2):

        @pl.when(r == k)
        def _():
            raw[0] = lp_ref[pl.ds(k, nb, stride=2), :]
            raw[1] = lb_ref[pl.ds(k, nb, stride=2), :]

    greetings = jnp.where(c == 0, 0, 2) + jnp.where(c == 1, 0, 2)
    pl.semaphore_wait(barrier, n_row - 1 + jnp.where(is_worker, greetings, 0))

    def cb_copy(i, row):
        return remote(pan.at[i], cb, cb_send.at[i], cb_recv, row, c)

    for i in range(R):
        src_col, src_row = slot_source(i)

        @pl.when((src_col == c) & (src_row != r))
        def _():
            cb_copy(i, src_row).start()

        @pl.when((src_col == c) & (src_row == r))
        def _():
            cb[...] = pan[i]

    def l_copy(d):
        return remote(
            pan.at[0, 0], l10, l_send.at[d], l_recv, lax.rem(r + d, n_row), c
        )

    def raw_copy():
        return remote(raw, raw1, raw_sem.at[0], raw_sem.at[1], 0, c)

    @pl.when(r == 1)
    def _():
        raw_copy().start()
        for d in range(1, n_row):
            l_copy(d).start()
        l10[...] = pan[0, 0]
        raw1[...] = raw[...]

    ct = jnp.concatenate(
        [jnp.concatenate([pan[i, k] for i in range(R)], axis=0) for k in range(2)],
        axis=1,
    ).T

    def p_copy(d, w):
        return remote(
            pbuf.at[d], recv.at[r], p_send.at[d], p_recv.at[r], w * s, c
        )

    def p_step(d):
        w = lax.rem(wk + 1 + d, T)
        block = h_ref[pl.ds(w, R * nb, stride=T), :]
        part = dot(ct, block)

        @pl.when(w * s != r)
        def _():
            pbuf[d] = part
            p_copy(d, w).start()

        @pl.when(w * s == r)
        def _():
            recv[r] = part

    for d in range(T):
        p_step(d)

    out_ref[...] = h_ref[...]

    @pl.when(is_worker)
    def _():
        acc = recv[r]
        for d in range(1, n_row):
            other = lax.rem(r + n_row - d, n_row)
            remote(
                pbuf.at[0], recv.at[other], p_send.at[0], p_recv.at[other], r, c
            ).wait_recv()
            acc = acc + recv[other]

        @pl.when(dst_row != r)
        def _():
            cb_copy(0, r).wait_recv()

        z = []
        for k in range(2):
            value = cb[2 + k].T - 2.0 * acc[k * nb : (k + 1) * nb]
            z.append(jnp.where(tile > k, value, 0.0))
        gpart[0:nb] = dot(z[1], cb[1])
        gpart[nb : 2 * nb] = dot(z[1], cb[0])
        gpart[2 * nb : 3 * nb] = dot(z[0], cb[0])

        def ga_copy(d):
            w = lax.rem(wk + d, T)
            return remote(
                gpart.at[pl.ds(pl.multiple_of(w * piece, 8), piece)],
                grecv.at[wk],
                ga_send.at[d],
                ga_recv.at[wk],
                w * s,
                c,
            )

        for d in range(1, T):
            ga_copy(d).start()

        @pl.when(r != 1)
        def _():
            l_copy(1).wait_recv()

        y1 = dot(inv_ref[1], z[1], 0, 0)
        y0 = dot(inv_ref[0], z[0] - dot(l10[...], y1, 0, 0), 0, 0)
        y0, y1 = 0.5 * y0, 0.5 * y1
        ybuf[0] = y0
        ybuf[1] = y1
        ybuf[2] = y0.T
        ybuf[3] = y1.T

        def row_copy(k):
            return remote(
                ybuf.at[k], rowupd.at[wk], y_send.at[k], row_recv.at[wk], k, c
            )

        def col_copy(k):
            return remote(
                ybuf.at[2 + k],
                colupd.at[dst_slot],
                y_send.at[2 + k],
                col_recv.at[dst_slot],
                dst_row,
                k,
            )

        for k in range(2):
            own_col = (dst_row == r) & (c == k)

            @pl.when(r != k)
            def _():
                row_copy(k).start()

            @pl.when(r == k)
            def _():
                rowupd[wk] = ybuf[k]

            @pl.when(jnp.logical_not(own_col))
            def _():
                col_copy(k).start()

            @pl.when(own_col)
            def _():
                colupd[dst_slot] = ybuf[2 + k]

        total = gpart[pl.ds(pl.multiple_of(wk * piece, 8), piece)]
        for d in range(1, T):
            other = lax.rem(wk + T - d, T)
            remote(
                gpart.at[pl.ds(0, piece)],
                grecv.at[other],
                ga_send.at[0],
                ga_recv.at[other],
                r,
                c,
            ).wait_recv()
            total = total + grecv[other]
        gred[...] = total

        def gb_copy(k, source):
            return remote(
                gred, g2.at[source], gb_send.at[k], gb_recv.at[source], r, k
            )

        for k in range(2):

            @pl.when(c != k)
            def _():
                gb_copy(k, c).start()

        @pl.when(c < 2)
        def _():
            summed = gred[...]
            for d in range(1, n_col):
                other = lax.rem(c + d, n_col)
                gb_copy(0, other).wait_recv()
                summed = summed + g2[other]
            gsum[...] = summed

            def gc_copy(k):
                return remote(
                    gsum, g3.at[wk], gc_send.at[k], gc_recv.at[wk], k, c
                )

            for k in range(2):

                @pl.when(r != k)
                def _():
                    gc_copy(k).start()

                @pl.when(r == k)
                def _():
                    g3[wk] = gsum[...]

            for k in range(2):

                @pl.when(r != k)
                def _():
                    gc_copy(k).wait_send()

        for d in range(1, T):
            ga_copy(d).wait_send()
        for k in range(2):

            @pl.when(r != k)
            def _():
                row_copy(k).wait_send()

            @pl.when(jnp.logical_not((dst_row == r) & (c == k)))
            def _():
                col_copy(k).wait_send()

            @pl.when(c != k)
            def _():
                gb_copy(k, c).wait_send()

    @pl.when(jnp.logical_not(is_worker) & (r != 1))
    def _():
        l_copy(1).wait_recv()

    @pl.when(r == 0)
    def _():
        raw_copy().wait_recv()

    @pl.when(c < 2)
    def _():
        for i in range(R):
            src_col, src_row = slot_source(i)

            @pl.when(jnp.logical_not((src_col == c) & (src_row == r)))
            def _():
                remote(
                    ybuf.at[0], colupd.at[i], y_send.at[0], col_recv.at[i], r, c
                ).wait_recv()

            at = pl.ds(i * nb * T, nb, stride=T)
            out_ref[at, :] = out_ref[at, :] + colupd[i]

    @pl.when(r < 2)
    def _():
        for t in range(T):

            @pl.when(t * s != r)
            def _():
                remote(
                    ybuf.at[0], rowupd.at[t], y_send.at[0], row_recv.at[t], r, c
                ).wait_recv()

            at = pl.ds(t, nb, stride=T)
            out_ref[at, :] = out_ref[at, :] + rowupd[t]

    @pl.when((r < 2) & (c < 2))
    def _():
        for w in range(T):

            @pl.when(w * s != r)
            def _():
                remote(
                    gsum, g3.at[w], gc_send.at[0], gc_recv.at[w], r, c
                ).wait_recv()

        gram = g3[...].reshape(3 * nb, nb)
        inv0, inv1, off = inv_ref[0], inv_ref[1], l10[...]
        g1 = dot(inv1, gram[0:nb], 0, 0)
        cross = dot(inv1, gram[nb : 2 * nb], 0, 0)
        s1 = diagonal_adjoint(raw1[0], raw1[1], g1, inv1)
        extra = cross + 2.0 * dot(s1, off)
        at = pl.ds(0, nb, stride=T)

        @pl.when((r == 1) & (c == 1))
        def _():
            out_ref[at, :] = out_ref[at, :] + s1

        @pl.when((r == 1) & (c == 0))
        def _():
            out_ref[at, :] = out_ref[at, :] - 0.5 * dot(extra, inv0)

        @pl.when((r == 0) & (c == 1))
        def _():
            out_ref[at, :] = out_ref[at, :] - 0.5 * dot(extra, inv0).T

        @pl.when((r == 0) & (c == 0))
        def _():
            inner = gram[2 * nb : 3 * nb] - dot(off, cross, 0, 0) - dot(extra, off, 0, 0)
            g0 = dot(inv0, inner, 0, 0)
            s0 = diagonal_adjoint(raw[0], raw[1], g0, inv0)
            out_ref[at, :] = out_ref[at, :] + s0

    for i in range(R):
        src_col, src_row = slot_source(i)

        @pl.when((src_col == c) & (src_row != r))
        def _():
            cb_copy(i, src_row).wait_send()

    @pl.when(r == 1)
    def _():
        raw_copy().wait_send()
        for d in range(1, n_row):
            l_copy(d).wait_send()

    for d in range(T):
        w = lax.rem(wk + 1 + d, T)

        @pl.when(w * s != r)
        def _():
            p_copy(d, w).wait_send()


def per_device(n_row, n_col, trail_adjoint, factor_panels, factor_adjoint, diag_inverse):
    R, _, nb, T, _, _ = trail_adjoint.shape
    f32 = jnp.float32
    piece = 3 * nb // T
    dma = pltpu.SemaphoreType.DMA
    vmem = pl.BlockSpec(memory_space=pltpu.VMEM)
    out = pl.pallas_call(
        functools.partial(kernel, (n_row, n_col, R, T, nb)),
        out_shape=jax.ShapeDtypeStruct((R * nb * T, nb), f32),
        in_specs=[vmem] * 4,
        out_specs=vmem,
        scratch_shapes=[
            pltpu.VMEM((R, 4, nb, nb), f32),
            pltpu.VMEM((2, nb, nb), f32),
            pltpu.VMEM((2, nb, nb), f32),
            pltpu.VMEM((nb, nb), f32),
            pltpu.VMEM((4, nb, nb), f32),
            pltpu.VMEM((T, 2 * nb, nb), f32),
            pltpu.VMEM((n_row, 2 * nb, nb), f32),
            pltpu.VMEM((3 * nb, nb), f32),
            pltpu.VMEM((T, piece, nb), f32),
            pltpu.VMEM((piece, nb), f32),
            pltpu.VMEM((n_col, piece, nb), f32),
            pltpu.VMEM((piece, nb), f32),
            pltpu.VMEM((T, piece, nb), f32),
            pltpu.VMEM((4, nb, nb), f32),
            pltpu.VMEM((T, nb, nb), f32),
            pltpu.VMEM((R, nb, nb), f32),
            dma((R,)),
            dma,
            dma((n_row,)),
            dma,
            dma((2,)),
            dma((T,)),
            dma((n_row,)),
            dma((T,)),
            dma((T,)),
            dma((2,)),
            dma((n_col,)),
            dma((2,)),
            dma((T,)),
            dma((4,)),
            dma((T,)),
            dma((R,)),
        ],
        compiler_params=pltpu.CompilerParams(
            collective_id=0, has_side_effects=True, vmem_limit_bytes=40 << 20
        ),
    )(
        trail_adjoint.reshape(R * nb * T, nb),
        factor_panels.reshape(R * nb * 2, nb),
        factor_adjoint.reshape(R * nb * 2, nb),
        diag_inverse,
    )
    return out.reshape(trail_adjoint.shape)


def solution(mesh):
    placed = (
        P(None, "row", None, None, "col", None),
        P(None, "row", None, None, None),
        P(None, "row", None, None, None),
        P(),
    )
    return jax.shard_map(
        functools.partial(per_device, mesh.shape["row"], mesh.shape["col"]),
        mesh=mesh,
        in_specs=placed,
        out_specs=P(None, "row", None, None, "col", None),
        check_vma=False,
    )
```

time: 333 us -> 48.9 us (0.15)
  waiting for transfers between devices: 284 us -> 0 us
  Pallas kernels: 0 us -> 42.7 us
  matrix products: 14.9 us -> 0 us
  between operations: 13.7 us -> 0.01 us
  local copies, waits for them, and re-layouts: 13 us -> 5.9 us
  other arithmetic: 6.17 us -> 0 us
    psum x4 -> x0, waiting for transfers between devices: 172 us -> none  [the longest x2 105 us: column_total(): return lax.psum(values, 'row')]
    all_gather x4 -> x0, waiting for transfers between devices: 111 us -> none  [to_columns(): lax.all_gather(values.reshape(local_tiles, 1, tile_size, breadth), 'row',...]
    pallas_call x0 -> x1, Pallas kernels: none -> 42.7 us  [per_device(): pl.pallas_call(functools.partial(kernel, (n_row, n_col, R, T, nb)), out_s...]
    dot_general x12 -> x0, matrix products: 14.9 us -> none  [product(): jnp.dot(left_matrix, right_matrix, precision=lax.Precision.HIGHEST, prefe...]
    select_n x3 -> x0, other arithmetic: 3.97 us -> none  [the longest x2 2.97 us: per_device(): jnp.where(owner_row, 0.5 * scaled_cols.T, 0.0)]
    unnamed x18 -> x9, local copies, waits for them, and re-layouts: 7.64 us -> 5.9 us
  transfers between devices with their start and end apart: 8 -> 0, of which waited for: 8 -> 0; matrix products, arithmetic and copies ran while one was open for 4% -> 0% of each run, Pallas kernels for 0% -> 0%
where the time goes in v1:
time: 48.9 us; the launch traced here: 48.6 us
  Pallas kernels  42.7 us (87%)
  local copies, waits for them, and re-layouts  5.9 us (12%)
    pallas_call x1, Pallas kernels, per_device(): pl.pallas_call(functools.partial(kernel, (n_row, n_col, R, T, nb)), out_s...  42.7 us
    unnamed x9, local copies, waits for them, and re-layouts  5.9 us

profile of v1, /device:TPU:0, one launch (start us, length us, event | category | flops | bytes accessed | tf_op | source)
XLA Modules:
  0.0 48.6 jit_solution(15669720362680993474)
XLA Ops:
  0.0 0.0 copy-start
  0.0 1.6 %copy-done = f32[4,1,128,8,1,128]{5,4,3,2,1,0:T(1,128)S(1)} copy-done((f32[4,1,128,8,1,128]{5,4,3,2,1,0:T(1,128)S(1)}, f32[4,1,128,8,1,128]{5,4,3,2,1,0:T(1,128)}, u32[]{:S(2)}) %copy-start) | copy-done | bytes 2097176
  1.6 0.0 copy-start.1
  1.6 1.0 %copy-done.1 = f32[4,1,128,2,128]{4,3,2,1,0:T(2,128)S(1)} copy-done((f32[4,1,128,2,128]{4,3,2,1,0:T(2,128)S(1)}, f32[4,1,128,2,128]{4,3,2,1,0:T(2,128)}, u32[]{:S(2)}) %copy-start.1) | copy-done | bytes 524312
  2.6 0.0 copy-start.2
  2.6 1.0 %copy-done.2 = f32[4,1,128,2,128]{4,3,2,1,0:T(2,128)S(1)} copy-done((f32[4,1,128,2,128]{4,3,2,1,0:T(2,128)S(1)}, f32[4,1,128,2,128]{4,3,2,1,0:T(2,128)}, u32[]{:S(2)}) %copy-start.2) | copy-done | bytes 524312
  3.7 0.0 copy-start.3
  3.7 0.9 %copy-done.3 = f32[2,128,128]{2,1,0:T(8,128)S(1)} copy-done((f32[2,128,128]{2,1,0:T(8,128)S(1)}, f32[2,128,128]{2,1,0:T(8,128)}, u32[]{:S(2)}) %copy-start.3) | copy-done | bytes 131096
  4.6 42.7 %shard_map.46 = f32[4096,128]{1,0:T(8,128)S(1)} custom-call(f32[4096,128]{1,0:T(8,128)S(1)} %bitcast.7, f32[1024,128]{1,0:T(8,128)S(1)} %bitcast.8, f32[1024,128]{1,0:T(8,128)S(1)} %bitcast.9, f32[2,128,128]{2,1,0:T(8,128)S(1)} %copy-done.3), custom_call_target="tpu_custom_call" | custom-call | tf_op jit(solution)/shard_map/pallas_call | solution.py:461
  47.3 1.3 %copy.7 = f32[4,1,128,8,1,128]{5,4,3,2,1,0:T(1,128)} copy(f32[4,1,128,8,1,128]{5,4,3,2,1,0:T(1,128)S(1)} %bitcast.6) | data formatting | bytes 4194304
Async XLA Ops:
  0.0 1.6 %copy-start = (f32[4,1,128,8,1,128]{5,4,3,2,1,0:T(1,128)S(1)}, f32[4,1,128,8,1,128]{5,4,3,2,1,0:T(1,128)}, u32[]{:S(2)}) copy-start(f32[4,1,128,8,1,128]{5,4,3,2,1,0:T(1,128)} %param.4) | copy-start | bytes 6291460
  1.6 1.0 %copy-start.1 = (f32[4,1,128,2,128]{4,3,2,1,0:T(2,128)S(1)}, f32[4,1,128,2,128]{4,3,2,1,0:T(2,128)}, u32[]{:S(2)}) copy-start(f32[4,1,128,2,128]{4,3,2,1,0:T(2,128)} %param.5) | copy-start | bytes 1572868
  2.6 1.0 %copy-start.2 = (f32[4,1,128,2,128]{4,3,2,1,0:T(2,128)S(1)}, f32[4,1,128,2,128]{4,3,2,1,0:T(2,128)}, u32[]{:S(2)}) copy-start(f32[4,1,128,2,128]{4,3,2,1,0:T(2,128)} %param.6) | copy-start | bytes 1572868
  3.7 0.9 %copy-start.3 = (f32[2,128,128]{2,1,0:T(8,128)S(1)}, f32[2,128,128]{2,1,0:T(8,128)}, u32[]{:S(2)}) copy-start(f32[2,128,128]{2,1,0:T(8,128)} %inv_ref.1) | copy-start | bytes 393220

commit v2 on v1

--- a/solution.py
+++ b/solution.py
@@ -10,14 +10,28 @@
 MESH = pl.DeviceIdType.MESH
 
 
-def dot(a, b, ca=1, cb=0):
-    return lax.dot_general(
-        a,
-        b,
-        (((ca,), (cb,)), ((), ())),
-        precision=lax.Precision.HIGHEST,
-        preferred_element_type=jnp.float32,
-    )
+def split(x):
+    high = x.astype(jnp.bfloat16)
+    low = (x - high.astype(jnp.float32)).astype(jnp.bfloat16)
+    return high, low
+
+
+def left_parts(a):
+    high, low = split(a)
+    return jnp.concatenate([high, high, low], axis=1)
+
+
+def right_parts(b):
+    high, low = split(b)
+    return jnp.concatenate([high, low, high], axis=0)
+
+
+def dot_parts(left, right):
+    return jnp.dot(left, right, preferred_element_type=jnp.float32)
+
+
+def dot(a, b):
+    return dot_parts(left_parts(a), right_parts(b))
 
 
 def halved_lower(matrix):
@@ -32,19 +46,26 @@
     return jnp.where(rows >= cols, matrix, 0.0)
 
 
-def diagonal_adjoint(lower_block, given_block, gram_block, inverse):
-    inner = halved_lower(dot(lower_block, lower(given_block - gram_block), 0, 0))
-    mixed = dot(dot(inverse, inner, 0, 0), inverse)
+def inner_block(lower_block, given_block, gram_block):
+    return halved_lower(dot(lower_block.T, lower(given_block - gram_block)))
+
+
+def mixed_block(inner, inverse):
+    mixed = dot(dot(inverse.T, inner), inverse)
     return 0.5 * (mixed + mixed.T)
 
 
 def kernel(
     sizes,
-    h_ref,
+    h_hbm,
+    lp_hbm,
+    lb_hbm,
+    inv_hbm,
+    out_ref,
     lp_ref,
     lb_ref,
     inv_ref,
-    out_ref,
+    pre,
     pan,
     raw,
     raw1,
@@ -77,6 +98,9 @@
     y_send,
     row_recv,
     col_recv,
+    in_sem,
+    pre_send,
+    pre_recv,
 ):
     n_row, n_col, R, T, nb = sizes
     s = n_row // T
@@ -84,7 +108,11 @@
     r = lax.axis_index("row")
     c = lax.axis_index("col")
     wk = r // s
-    is_worker = lax.rem(r, s) == 0
+
+    def wrow(t):
+        return t * s + (s - 1) * (t % 2 if isinstance(t, int) else lax.rem(t, 2))
+
+    is_worker = wrow(wk) == r
     tile = wk * n_col + c
     dst_row = lax.rem(tile, n_row)
     dst_slot = tile // n_row
@@ -101,7 +129,16 @@
 
     def slot_source(i):
         g = i * n_row + r
-        return lax.rem(g, n_col), (g // n_col) * s
+        return lax.rem(g, n_col), wrow(g // n_col)
+
+    reads = [
+        pltpu.make_async_copy(source, target, in_sem.at[i])
+        for i, (source, target) in enumerate(
+            [(lp_hbm, lp_ref), (lb_hbm, lb_ref), (inv_hbm, inv_ref), (h_hbm, out_ref)]
+        )
+    ]
+    for read in reads:
+        read.start()
 
     barrier = pltpu.get_barrier_semaphore()
     for d in range(1, n_row):
@@ -126,6 +163,9 @@
                     pl.semaphore_signal(
                         barrier, inc=1, device_id=(r, other), device_id_type=MESH
                     )
+
+    for read in reads[:2]:
+        read.wait()
 
     for i in range(R):
         for k in range(2):
@@ -181,36 +221,63 @@
         [jnp.concatenate([pan[i, k] for i in range(R)], axis=0) for k in range(2)],
         axis=1,
     ).T
-
-    def p_copy(d, w):
+    ct = left_parts(ct)
+    half = T // 2
+    side = lax.rem(r, 2)
+    partner = r + 1 - 2 * side
+
+    def partial(t):
+        return dot_parts(ct, right_parts(out_ref[pl.ds(t, R * nb, stride=T), :]))
+
+    def pair(d):
+        return lax.rem(wk // 2 + 1 + d, half)
+
+    def pre_copy(d):
         return remote(
-            pbuf.at[d], recv.at[r], p_send.at[d], p_recv.at[r], w * s, c
+            pbuf.at[d],
+            pre.at[pair(d)],
+            pre_send.at[d],
+            pre_recv.at[pair(d)],
+            partner,
+            c,
         )
 
-    def p_step(d):
-        w = lax.rem(wk + 1 + d, T)
-        block = h_ref[pl.ds(w, R * nb, stride=T), :]
-        part = dot(ct, block)
-
-        @pl.when(w * s != r)
-        def _():
-            pbuf[d] = part
-            p_copy(d, w).start()
-
-        @pl.when(w * s == r)
-        def _():
-            recv[r] = part
-
-    for d in range(T):
-        p_step(d)
-
-    out_ref[...] = h_ref[...]
+    def p_copy(d):
+        return remote(
+            pbuf.at[half + d],
+            recv.at[r // 2],
+            p_send.at[d],
+            p_recv.at[r // 2],
+            wrow(2 * pair(d) + side),
+            c,
+        )
+
+    for read in reads[2:]:
+        read.wait()
+
+    for d in range(half):
+        pbuf[d] = partial(2 * pair(d) + 1 - side)
+        pre_copy(d).start()
+    for d in range(half):
+        t = 2 * pair(d) + side
+        part = partial(t)
+        pre_copy(d).wait_recv()
+        part = part + pre[pair(d)]
+
+        @pl.when(wrow(t) != r)
+        def _():
+            pbuf[half + d] = part
+            p_copy(d).start()
+
+        @pl.when(wrow(t) == r)
+        def _():
+            recv[r // 2] = part
 
     @pl.when(is_worker)
     def _():
-        acc = recv[r]
-        for d in range(1, n_row):
-            other = lax.rem(r + n_row - d, n_row)
+        acc = recv[r // 2]
+        for d in range(1, n_row // 2):
+            other = lax.rem(r // 2 + n_row // 2 - d, n_row // 2)
             remote(
                 pbuf.at[0], recv.at[other], p_send.at[0], p_recv.at[other], r, c
             ).wait_recv()
@@ -235,7 +302,7 @@
                 grecv.at[wk],
                 ga_send.at[d],
                 ga_recv.at[wk],
-                w * s,
+                wrow(w),
                 c,
             )
 
@@ -246,8 +313,8 @@
         def _():
             l_copy(1).wait_recv()
 
-        y1 = dot(inv_ref[1], z[1], 0, 0)
-        y0 = dot(inv_ref[0], z[0] - dot(l10[...], y1, 0, 0), 0, 0)
+        y1 = dot(inv_ref[1].T, z[1])
+        y0 = dot(inv_ref[0].T, z[0] - dot(l10[...].T, y1))
         y0, y1 = 0.5 * y0, 0.5 * y1
         ybuf[0] = y0
         ybuf[1] = y1
@@ -268,25 +335,6 @@
                 dst_row,
                 k,
             )
-
-        for k in range(2):
-            own_col = (dst_row == r) & (c == k)
-
-            @pl.when(r != k)
-            def _():
-                row_copy(k).start()
-
-            @pl.when(r == k)
-            def _():
-                rowupd[wk] = ybuf[k]
-
-            @pl.when(jnp.logical_not(own_col))
-            def _():
-                col_copy(k).start()
-
-            @pl.when(own_col)
-            def _():
-                colupd[dst_slot] = ybuf[2 + k]
 
         total = gpart[pl.ds(pl.multiple_of(wk * piece, 8), piece)]
         for d in range(1, T):
@@ -343,6 +391,25 @@
                 def _():
                     gc_copy(k).wait_send()
 
+        for k in range(2):
+            own_col = (dst_row == r) & (c == k)
+
+            @pl.when(r != k)
+            def _():
+                row_copy(k).start()
+
+            @pl.when(r == k)
+            def _():
+                rowupd[wk] = ybuf[k]
+
+            @pl.when(jnp.logical_not(own_col))
+            def _():
+                col_copy(k).start()
+
+            @pl.when(own_col)
+            def _():
+                colupd[dst_slot] = ybuf[2 + k]
+
         for d in range(1, T):
             ga_copy(d).wait_send()
         for k in range(2):
@@ -385,7 +452,7 @@
     def _():
         for t in range(T):
 
-            @pl.when(t * s != r)
+            @pl.when(wrow(t) != r)
             def _():
                 remote(
                     ybuf.at[0], rowupd.at[t], y_send.at[0], row_recv.at[t], r, c
@@ -398,7 +465,7 @@
     def _():
         for w in range(T):
 
-            @pl.when(w * s != r)
+            @pl.when(wrow(w) != r)
             def _():
                 remote(
                     gsum, g3.at[w], gc_send.at[0], gc_recv.at[w], r, c
@@ -406,30 +473,37 @@
 
         gram = g3[...].reshape(3 * nb, nb)
         inv0, inv1, off = inv_ref[0], inv_ref[1], l10[...]
-        g1 = dot(inv1, gram[0:nb], 0, 0)
-        cross = dot(inv1, gram[nb : 2 * nb], 0, 0)
-        s1 = diagonal_adjoint(raw1[0], raw1[1], g1, inv1)
-        extra = cross + 2.0 * dot(s1, off)
+        g1 = dot(inv1.T, gram[0:nb])
+        p1 = inner_block(raw1[0], raw1[1], g1)
+        cross = dot(inv1.T, gram[nb : 2 * nb])
         at = pl.ds(0, nb, stride=T)
 
         @pl.when((r == 1) & (c == 1))
         def _():
-            out_ref[at, :] = out_ref[at, :] + s1
-
-        @pl.when((r == 1) & (c == 0))
-        def _():
-            out_ref[at, :] = out_ref[at, :] - 0.5 * dot(extra, inv0)
-
-        @pl.when((r == 0) & (c == 1))
-        def _():
-            out_ref[at, :] = out_ref[at, :] - 0.5 * dot(extra, inv0).T
+            out_ref[at, :] = out_ref[at, :] + mixed_block(p1, inv1)
+
+        @pl.when(r + c == 1)
+        def _():
+            moved = dot(inv1, dot(off, inv0))
+            base = dot(cross, inv0)
+            change = 0.5 * base + 0.5 * dot(inv1.T, dot(p1 + p1.T, moved))
+
+            @pl.when(c == 0)
+            def _():
+                out_ref[at, :] = out_ref[at, :] - change
+
+            @pl.when(c == 1)
+            def _():
+                out_ref[at, :] = out_ref[at, :] - change.T
 
         @pl.when((r == 0) & (c == 0))
         def _():
-            inner = gram[2 * nb : 3 * nb] - dot(off, cross, 0, 0) - dot(extra, off, 0, 0)
-            g0 = dot(inv0, inner, 0, 0)
-            s0 = diagonal_adjoint(raw[0], raw[1], g0, inv0)
-            out_ref[at, :] = out_ref[at, :] + s0
+            moved = dot(inv1, off)
+            tied = dot(off.T, cross)
+            base = dot(inv0.T, gram[2 * nb : 3 * nb] - tied - tied.T)
+            g0 = base - dot(dot(moved, inv0).T, dot(p1 + p1.T, moved))
+            p0 = inner_block(raw[0], raw[1], g0)
+            out_ref[at, :] = out_ref[at, :] + mixed_block(p0, inv0)
 
     for i in range(R):
         src_col, src_row = slot_source(i)
@@ -444,12 +518,12 @@
         for d in range(1, n_row):
             l_copy(d).wait_send()
 
-    for d in range(T):
-        w = lax.rem(wk + 1 + d, T)
-
-        @pl.when(w * s != r)
-        def _():
-            p_copy(d, w).wait_send()
+    for d in range(half):
+        pre_copy(d).wait_send()
+
+        @pl.when(wrow(2 * pair(d) + side) != r)
+        def _():
+            p_copy(d).wait_send()
 
 
 def per_device(n_row, n_col, trail_adjoint, factor_panels, factor_adjoint, diag_inverse):
@@ -461,16 +535,20 @@
     out = pl.pallas_call(
         functools.partial(kernel, (n_row, n_col, R, T, nb)),
         out_shape=jax.ShapeDtypeStruct((R * nb * T, nb), f32),
-        in_specs=[vmem] * 4,
+        in_specs=[pl.BlockSpec(memory_space=pl.ANY)] * 4,
         out_specs=vmem,
         scratch_shapes=[
+            pltpu.VMEM((R * nb * 2, nb), f32),
+            pltpu.VMEM((R * nb * 2, nb), f32),
+            pltpu.VMEM((2, nb, nb), f32),
+            pltpu.VMEM((T // 2, 2 * nb, nb), f32),
             pltpu.VMEM((R, 4, nb, nb), f32),
             pltpu.VMEM((2, nb, nb), f32),
             pltpu.VMEM((2, nb, nb), f32),
             pltpu.VMEM((nb, nb), f32),
             pltpu.VMEM((4, nb, nb), f32),
             pltpu.VMEM((T, 2 * nb, nb), f32),
-            pltpu.VMEM((n_row, 2 * nb, nb), f32),
+            pltpu.VMEM((n_row // 2, 2 * nb, nb), f32),
             pltpu.VMEM((3 * nb, nb), f32),
             pltpu.VMEM((T, piece, nb), f32),
             pltpu.VMEM((piece, nb), f32),
@@ -485,8 +563,8 @@
             dma((n_row,)),
             dma,
             dma((2,)),
-            dma((T,)),
-            dma((n_row,)),
+            dma((T // 2,)),
+            dma((n_row // 2,)),
             dma((T,)),
             dma((T,)),
             dma((2,)),
@@ -496,9 +574,12 @@
             dma((4,)),
             dma((T,)),
             dma((R,)),
+            dma((4,)),
+            dma((T // 2,)),
+            dma((T // 2,)),
         ],
         compiler_params=pltpu.CompilerParams(
-            collective_id=0, has_side_effects=True, vmem_limit_bytes=40 << 20
+            collective_id=0, has_side_effects=True, vmem_limit_bytes=48 << 20
         ),
     )(
         trail_adjoint.reshape(R * nb * T, nb),

time: 48.9 us -> 49.3 us (level)
  no operation moved by 1% of the time
where the time goes in v2:
time: 49.3 us; the launch traced here: 49 us
  Pallas kernels  43.1 us (87%)
  local copies, waits for them, and re-layouts  5.9 us (12%)
    pallas_call x1, Pallas kernels, per_device(): pl.pallas_call(functools.partial(kernel, (n_row, n_col, R, T, nb)), out_s...  43.1 us
    unnamed x9, local copies, waits for them, and re-layouts  5.9 us

profile of v2, /device:TPU:0, one launch (start us, length us, event | category | flops | bytes accessed | tf_op | source)
XLA Modules:
  0.0 49.0 jit_solution(9354496905382446351)
XLA Ops:
  0.0 0.0 copy-start
  0.0 1.6 %copy-done = f32[4,1,128,8,1,128]{5,4,3,2,1,0:T(1,128)S(1)} copy-done((f32[4,1,128,8,1,128]{5,4,3,2,1,0:T(1,128)S(1)}, f32[4,1,128,8,1,128]{5,4,3,2,1,0:T(1,128)}, u32[]{:S(2)}) %copy-start) | copy-done | bytes 2097176
  1.6 0.0 copy-start.1
  1.6 1.0 %copy-done.1 = f32[4,1,128,2,128]{4,3,2,1,0:T(2,128)S(1)} copy-done((f32[4,1,128,2,128]{4,3,2,1,0:T(2,128)S(1)}, f32[4,1,128,2,128]{4,3,2,1,0:T(2,128)}, u32[]{:S(2)}) %copy-start.1) | copy-done | bytes 524312
  2.6 0.0 copy-start.2
  2.6 1.0 %copy-done.2 = f32[4,1,128,2,128]{4,3,2,1,0:T(2,128)S(1)} copy-done((f32[4,1,128,2,128]{4,3,2,1,0:T(2,128)S(1)}, f32[4,1,128,2,128]{4,3,2,1,0:T(2,128)}, u32[]{:S(2)}) %copy-start.2) | copy-done | bytes 524312
  3.7 0.0 copy-start.3
  3.7 0.9 %copy-done.3 = f32[2,128,128]{2,1,0:T(8,128)S(1)} copy-done((f32[2,128,128]{2,1,0:T(8,128)S(1)}, f32[2,128,128]{2,1,0:T(8,128)}, u32[]{:S(2)}) %copy-start.3) | copy-done | bytes 131096
  4.6 43.1 %shard_map.46 = f32[4096,128]{1,0:T(8,128)S(1)} custom-call(f32[4096,128]{1,0:T(8,128)S(1)} %bitcast.7, f32[1024,128]{1,0:T(8,128)S(1)} %bitcast.8, f32[1024,128]{1,0:T(8,128)S(1)} %bitcast.9, f32[2,128,128]{2,1,0:T(8,128)S(1)} %copy-done.3), custom_call_target="tpu_custom_call" | custom-call | tf_op jit(solution)/shard_map/pallas_call | solution.py:535
  47.7 1.3 %copy.7 = f32[4,1,128,8,1,128]{5,4,3,2,1,0:T(1,128)} copy(f32[4,1,128,8,1,128]{5,4,3,2,1,0:T(1,128)S(1)} %bitcast.6) | data formatting | bytes 4194304
Async XLA Ops:
  0.0 1.6 %copy-start = (f32[4,1,128,8,1,128]{5,4,3,2,1,0:T(1,128)S(1)}, f32[4,1,128,8,1,128]{5,4,3,2,1,0:T(1,128)}, u32[]{:S(2)}) copy-start(f32[4,1,128,8,1,128]{5,4,3,2,1,0:T(1,128)} %param.4) | copy-start | bytes 6291460
  1.6 1.0 %copy-start.1 = (f32[4,1,128,2,128]{4,3,2,1,0:T(2,128)S(1)}, f32[4,1,128,2,128]{4,3,2,1,0:T(2,128)}, u32[]{:S(2)}) copy-start(f32[4,1,128,2,128]{4,3,2,1,0:T(2,128)} %param.5) | copy-start | bytes 1572868
  2.6 1.0 %copy-start.2 = (f32[4,1,128,2,128]{4,3,2,1,0:T(2,128)S(1)}, f32[4,1,128,2,128]{4,3,2,1,0:T(2,128)}, u32[]{:S(2)}) copy-start(f32[4,1,128,2,128]{4,3,2,1,0:T(2,128)} %param.6) | copy-start | bytes 1572868
  3.7 0.9 %copy-start.3 = (f32[2,128,128]{2,1,0:T(8,128)S(1)}, f32[2,128,128]{2,1,0:T(8,128)}, u32[]{:S(2)}) copy-start(f32[2,128,128]{2,1,0:T(8,128)} %inv_hbm.1) | copy-start | bytes 393220

commit v3 on v2

--- a/solution.py
+++ b/solution.py
@@ -434,33 +434,6 @@
     def _():
         raw_copy().wait_recv()
 
-    @pl.when(c < 2)
-    def _():
-        for i in range(R):
-            src_col, src_row = slot_source(i)
-
-            @pl.when(jnp.logical_not((src_col == c) & (src_row == r)))
-            def _():
-                remote(
-                    ybuf.at[0], colupd.at[i], y_send.at[0], col_recv.at[i], r, c
-                ).wait_recv()
-
-            at = pl.ds(i * nb * T, nb, stride=T)
-            out_ref[at, :] = out_ref[at, :] + colupd[i]
-
-    @pl.when(r < 2)
-    def _():
-        for t in range(T):
-
-            @pl.when(wrow(t) != r)
-            def _():
-                remote(
-                    ybuf.at[0], rowupd.at[t], y_send.at[0], row_recv.at[t], r, c
-                ).wait_recv()
-
-            at = pl.ds(t, nb, stride=T)
-            out_ref[at, :] = out_ref[at, :] + rowupd[t]
-
     @pl.when((r < 2) & (c < 2))
     def _():
         for w in range(T):
@@ -504,6 +477,33 @@
             g0 = base - dot(dot(moved, inv0).T, dot(p1 + p1.T, moved))
             p0 = inner_block(raw[0], raw[1], g0)
             out_ref[at, :] = out_ref[at, :] + mixed_block(p0, inv0)
+
+    @pl.when(c < 2)
+    def _():
+        for i in range(R):
+            src_col, src_row = slot_source(i)
+
+            @pl.when(jnp.logical_not((src_col == c) & (src_row == r)))
+            def _():
+                remote(
+                    ybuf.at[0], colupd.at[i], y_send.at[0], col_recv.at[i], r, c
+                ).wait_recv()
+
+            at = pl.ds(i * nb * T, nb, stride=T)
+            out_ref[at, :] = out_ref[at, :] + colupd[i]
+
+    @pl.when(r < 2)
+    def _():
+        for t in range(T):
+
+            @pl.when(wrow(t) != r)
+            def _():
+                remote(
+                    ybuf.at[0], rowupd.at[t], y_send.at[0], row_recv.at[t], r, c
+                ).wait_recv()
+
+            at = pl.ds(t, nb, stride=T)
+            out_ref[at, :] = out_ref[at, :] + rowupd[t]
 
     for i in range(R):
         src_col, src_row = slot_source(i)
@@ -535,7 +535,7 @@
     out = pl.pallas_call(
         functools.partial(kernel, (n_row, n_col, R, T, nb)),
         out_shape=jax.ShapeDtypeStruct((R * nb * T, nb), f32),
-        in_specs=[pl.BlockSpec(memory_space=pl.ANY)] * 4,
+        in_specs=[pl.BlockSpec(memory_space=pltpu.HBM)] * 4,
         out_specs=vmem,
         scratch_shapes=[
             pltpu.VMEM((R * nb * 2, nb), f32),

time: 49.3 us -> 47.6 us (0.966)
  Pallas kernels: 43.1 us -> 41.4 us
    pallas_call x1, Pallas kernels: 43.1 us -> 41.4 us  [per_device(): pl.pallas_call(functools.partial(kernel, (n_row, n_col, R, T, nb)), out_s...]
where the time goes in v3:
time: 47.6 us; the launch traced here: 47.3 us
  Pallas kernels  41.4 us (87%)
  local copies, waits for them, and re-layouts  5.9 us (12%)
    pallas_call x1, Pallas kernels, per_device(): pl.pallas_call(functools.partial(kernel, (n_row, n_col, R, T, nb)), out_s...  41.4 us
    unnamed x9, local copies, waits for them, and re-layouts  5.9 us

profile of v3, /device:TPU:0, one launch (start us, length us, event | category | flops | bytes accessed | tf_op | source)
XLA Modules:
  0.0 47.3 jit_solution(5023986768528359341)
XLA Ops:
  0.0 0.0 copy-start
  0.0 1.6 %copy-done = f32[4,1,128,8,1,128]{5,4,3,2,1,0:T(1,128)S(1)} copy-done((f32[4,1,128,8,1,128]{5,4,3,2,1,0:T(1,128)S(1)}, f32[4,1,128,8,1,128]{5,4,3,2,1,0:T(1,128)}, u32[]{:S(2)}) %copy-start) | copy-done | bytes 2097176
  1.6 0.0 copy-start.1
  1.6 1.0 %copy-done.1 = f32[4,1,128,2,128]{4,3,2,1,0:T(2,128)S(1)} copy-done((f32[4,1,128,2,128]{4,3,2,1,0:T(2,128)S(1)}, f32[4,1,128,2,128]{4,3,2,1,0:T(2,128)}, u32[]{:S(2)}) %copy-start.1) | copy-done | bytes 524312
  2.6 0.0 copy-start.2
  2.6 1.0 %copy-done.2 = f32[4,1,128,2,128]{4,3,2,1,0:T(2,128)S(1)} copy-done((f32[4,1,128,2,128]{4,3,2,1,0:T(2,128)S(1)}, f32[4,1,128,2,128]{4,3,2,1,0:T(2,128)}, u32[]{:S(2)}) %copy-start.2) | copy-done | bytes 524312
  3.7 0.0 copy-start.3
  3.7 0.9 %copy-done.3 = f32[2,128,128]{2,1,0:T(8,128)S(1)} copy-done((f32[2,128,128]{2,1,0:T(8,128)S(1)}, f32[2,128,128]{2,1,0:T(8,128)}, u32[]{:S(2)}) %copy-start.3) | copy-done | bytes 131096
  4.6 41.4 %shard_map.46 = f32[4096,128]{1,0:T(8,128)S(1)} custom-call(f32[4096,128]{1,0:T(8,128)S(1)} %bitcast.7, f32[1024,128]{1,0:T(8,128)S(1)} %bitcast.8, f32[1024,128]{1,0:T(8,128)S(1)} %bitcast.9, f32[2,128,128]{2,1,0:T(8,128)S(1)} %copy-done.3), custom_call_target="tpu_custom_call" | custom-call | tf_op jit(solution)/shard_map/pallas_call | solution.py:535
  46.0 1.3 %copy.7 = f32[4,1,128,8,1,128]{5,4,3,2,1,0:T(1,128)} copy(f32[4,1,128,8,1,128]{5,4,3,2,1,0:T(1,128)S(1)} %bitcast.6) | data formatting | bytes 4194304
Async XLA Ops:
  0.0 1.6 %copy-start = (f32[4,1,128,8,1,128]{5,4,3,2,1,0:T(1,128)S(1)}, f32[4,1,128,8,1,128]{5,4,3,2,1,0:T(1,128)}, u32[]{:S(2)}) copy-start(f32[4,1,128,8,1,128]{5,4,3,2,1,0:T(1,128)} %param.4) | copy-start | bytes 6291460
  1.6 1.0 %copy-start.1 = (f32[4,1,128,2,128]{4,3,2,1,0:T(2,128)S(1)}, f32[4,1,128,2,128]{4,3,2,1,0:T(2,128)}, u32[]{:S(2)}) copy-start(f32[4,1,128,2,128]{4,3,2,1,0:T(2,128)} %param.5) | copy-start | bytes 1572868
  2.6 1.0 %copy-start.2 = (f32[4,1,128,2,128]{4,3,2,1,0:T(2,128)S(1)}, f32[4,1,128,2,128]{4,3,2,1,0:T(2,128)}, u32[]{:S(2)}) copy-start(f32[4,1,128,2,128]{4,3,2,1,0:T(2,128)} %param.6) | copy-start | bytes 1572868
  3.7 0.9 %copy-start.3 = (f32[2,128,128]{2,1,0:T(8,128)S(1)}, f32[2,128,128]{2,1,0:T(8,128)}, u32[]{:S(2)}) copy-start(f32[2,128,128]{2,1,0:T(8,128)} %inv_hbm.1) | copy-start | bytes 393220

commit v4 on v3

--- a/solution.py
+++ b/solution.py
@@ -188,7 +188,7 @@
     pl.semaphore_wait(barrier, n_row - 1 + jnp.where(is_worker, greetings, 0))
 
     def cb_copy(i, row):
-        return remote(pan.at[i], cb, cb_send.at[i], cb_recv, row, c)
+        return remote(pan.at[i, pl.ds(0, 2)], cb, cb_send.at[i], cb_recv, row, c)
 
     for i in range(R):
         src_col, src_row = slot_source(i)
@@ -199,7 +199,8 @@
 
         @pl.when((src_col == c) & (src_row == r))
         def _():
-            cb[...] = pan[i]
+            cb[0] = pan[i, 0]
+            cb[1] = pan[i, 1]
 
     def l_copy(d):
         return remote(
@@ -208,14 +209,6 @@
 
     def raw_copy():
         return remote(raw, raw1, raw_sem.at[0], raw_sem.at[1], 0, c)
-
-    @pl.when(r == 1)
-    def _():
-        raw_copy().start()
-        for d in range(1, n_row):
-            l_copy(d).start()
-        l10[...] = pan[0, 0]
-        raw1[...] = raw[...]
 
     ct = jnp.concatenate(
         [jnp.concatenate([pan[i, k] for i in range(R)], axis=0) for k in range(2)],
@@ -255,23 +248,39 @@
     for read in reads[2:]:
         read.wait()
 
+    def fill(at, t):
+        pbuf[at] = partial(t)
+        g = t * n_col + c
+
+        @pl.when(lax.rem(g, n_row) == r)
+        def _():
+            given = jnp.concatenate([pan[g // n_row, 2 + k].T for k in range(2)], axis=0)
+            pbuf[at] = pbuf[at] - 0.5 * given
+
     for d in range(half):
-        pbuf[d] = partial(2 * pair(d) + 1 - side)
+        fill(d, 2 * pair(d) + 1 - side)
         pre_copy(d).start()
     for d in range(half):
         t = 2 * pair(d) + side
-        part = partial(t)
+        fill(half + d, t)
         pre_copy(d).wait_recv()
-        part = part + pre[pair(d)]
+        pbuf[half + d] = pbuf[half + d] + pre[pair(d)]
 
         @pl.when(wrow(t) != r)
         def _():
-            pbuf[half + d] = part
             p_copy(d).start()
 
         @pl.when(wrow(t) == r)
         def _():
-            recv[r // 2] = part
+            recv[r // 2] = pbuf[half + d]
+
+    @pl.when(r == 1)
+    def _():
+        raw_copy().start()
+        for d in range(1, n_row):
+            l_copy(d).start()
+        l10[...] = pan[0, 0]
+        raw1[...] = raw[...]
 
     @pl.when(is_worker)
     def _():
@@ -289,7 +298,7 @@
 
         z = []
         for k in range(2):
-            value = cb[2 + k].T - 2.0 * acc[k * nb : (k + 1) * nb]
+            value = -2.0 * acc[k * nb : (k + 1) * nb]
             z.append(jnp.where(tile > k, value, 0.0))
         gpart[0:nb] = dot(z[1], cb[1])
         gpart[nb : 2 * nb] = dot(z[1], cb[0])
@@ -546,7 +555,7 @@
             pltpu.VMEM((2, nb, nb), f32),
             pltpu.VMEM((2, nb, nb), f32),
             pltpu.VMEM((nb, nb), f32),
-            pltpu.VMEM((4, nb, nb), f32),
+            pltpu.VMEM((2, nb, nb), f32),
             pltpu.VMEM((T, 2 * nb, nb), f32),
             pltpu.VMEM((n_row // 2, 2 * nb, nb), f32),
             pltpu.VMEM((3 * nb, nb), f32),
@@ -579,7 +588,7 @@
             dma((T // 2,)),
         ],
         compiler_params=pltpu.CompilerParams(
-            collective_id=0, has_side_effects=True, vmem_limit_bytes=48 << 20
+            collective_id=0, has_side_effects=True, vmem_limit_bytes=58 << 20
         ),
     )(
         trail_adjoint.reshape(R * nb * T, nb),

time: 47.6 us -> 42.3 us (0.89)
  Pallas kernels: 41.4 us -> 37.8 us
  local copies, waits for them, and re-layouts: 5.9 us -> 4.35 us
    pallas_call x1, Pallas kernels: 41.4 us -> 37.8 us  [per_device(): pl.pallas_call(functools.partial(kernel, (n_row, n_col, R, T, nb)), out_s...]
    unnamed x9 -> x1, local copies, waits for them, and re-layouts: 5.9 us -> 4.35 us
where the time goes in v4:
time: 42.3 us; the launch traced here: 42.2 us
  Pallas kernels  37.8 us (89%)
  local copies, waits for them, and re-layouts  4.35 us (10%)
    pallas_call x1, Pallas kernels, per_device(): pl.pallas_call(functools.partial(kernel, (n_row, n_col, R, T, nb)), out_s...  37.8 us
    unnamed x1, local copies, waits for them, and re-layouts  4.35 us

profile of v4, /device:TPU:0, one launch (start us, length us, event | category | flops | bytes accessed | tf_op | source)
XLA Modules:
  0.0 42.2 jit_solution(91204288406755740)
XLA Ops:
  0.0 37.8 %shard_map.46 = f32[4096,128]{1,0:T(8,128)} custom-call(f32[4096,128]{1,0:T(8,128)} %bitcast.7, f32[1024,128]{1,0:T(8,128)} %bitcast.8, f32[1024,128]{1,0:T(8,128)} %bitcast.9, f32[2,128,128]{2,1,0:T(8,128)} %inv_hbm.1), custom_call_target="tpu_custom_call" | custom-call | tf_op jit(solution)/shard_map/pallas_call | solution.py:544
  37.8 4.3 %copy.7 = f32[4,1,128,8,1,128]{5,4,3,2,1,0:T(1,128)} copy(f32[4,1,128,8,1,128]{5,4,3,2,1,0:T(1,128)} %bitcast.6) | data formatting | bytes 4194304

commit v5 on v4

--- a/solution.py
+++ b/solution.py
@@ -588,7 +588,7 @@
             dma((T // 2,)),
         ],
         compiler_params=pltpu.CompilerParams(
-            collective_id=0, has_side_effects=True, vmem_limit_bytes=58 << 20
+            collective_id=0, has_side_effects=True, vmem_limit_bytes=50 << 20
         ),
     )(
         trail_adjoint.reshape(R * nb * T, nb),

time: 42.3 us -> 41.3 us (0.976)
  Pallas kernels: 37.8 us -> 36.7 us
    pallas_call x1, Pallas kernels: 37.8 us -> 36.7 us  [per_device(): pl.pallas_call(functools.partial(kernel, (n_row, n_col, R, T, nb)), out_s...]
    unnamed x1 -> x7, local copies, waits for them, and re-layouts: 4.35 us -> 4.31 us
where the time goes in v5:
time: 41.3 us; the launch traced here: 41 us
  Pallas kernels  36.7 us (89%)
  local copies, waits for them, and re-layouts  4.31 us (10%)
    pallas_call x1, Pallas kernels, per_device(): pl.pallas_call(functools.partial(kernel, (n_row, n_col, R, T, nb)), out_s...  36.7 us
    unnamed x7, local copies, waits for them, and re-layouts  4.31 us

profile of v5, /device:TPU:0, one launch (start us, length us, event | category | flops | bytes accessed | tf_op | source)
XLA Modules:
  0.0 41.0 jit_solution(17925812908577405827)
XLA Ops:
  0.0 0.0 copy-start
  0.0 1.0 %copy-done = f32[4,1,128,2,128]{4,3,2,1,0:T(2,128)S(1)} copy-done((f32[4,1,128,2,128]{4,3,2,1,0:T(2,128)S(1)}, f32[4,1,128,2,128]{4,3,2,1,0:T(2,128)}, u32[]{:S(2)}) %copy-start) | copy-done | bytes 524312
  1.0 0.0 copy-start.1
  1.0 1.0 %copy-done.1 = f32[4,1,128,2,128]{4,3,2,1,0:T(2,128)S(1)} copy-done((f32[4,1,128,2,128]{4,3,2,1,0:T(2,128)S(1)}, f32[4,1,128,2,128]{4,3,2,1,0:T(2,128)}, u32[]{:S(2)}) %copy-start.1) | copy-done | bytes 524312
  2.1 0.0 copy-start.2
  2.1 0.9 %copy-done.2 = f32[2,128,128]{2,1,0:T(8,128)S(1)} copy-done((f32[2,128,128]{2,1,0:T(8,128)S(1)}, f32[2,128,128]{2,1,0:T(8,128)}, u32[]{:S(2)}) %copy-start.2) | copy-done | bytes 131096
  3.0 36.7 %shard_map.46 = f32[4096,128]{1,0:T(8,128)S(1)} custom-call(f32[4096,128]{1,0:T(8,128)} %bitcast.9, f32[1024,128]{1,0:T(8,128)S(1)} %bitcast.7, f32[1024,128]{1,0:T(8,128)S(1)} %bitcast.8, f32[2,128,128]{2,1,0:T(8,128)S(1)} %copy-done.2), custom_call_target="tpu_custom_call" | custom-call | tf_op jit(solution)/shard_map/pallas_call | solution.py:544
  39.7 1.3 %copy.7 = f32[4,1,128,8,1,128]{5,4,3,2,1,0:T(1,128)} copy(f32[4,1,128,8,1,128]{5,4,3,2,1,0:T(1,128)S(1)} %bitcast.6) | data formatting | bytes 4194304
Async XLA Ops:
  0.0 1.0 %copy-start = (f32[4,1,128,2,128]{4,3,2,1,0:T(2,128)S(1)}, f32[4,1,128,2,128]{4,3,2,1,0:T(2,128)}, u32[]{:S(2)}) copy-start(f32[4,1,128,2,128]{4,3,2,1,0:T(2,128)} %param.5) | copy-start | bytes 1572868
  1.0 1.0 %copy-start.1 = (f32[4,1,128,2,128]{4,3,2,1,0:T(2,128)S(1)}, f32[4,1,128,2,128]{4,3,2,1,0:T(2,128)}, u32[]{:S(2)}) copy-start(f32[4,1,128,2,128]{4,3,2,1,0:T(2,128)} %param.6) | copy-start | bytes 1572868
  2.1 0.9 %copy-start.2 = (f32[2,128,128]{2,1,0:T(8,128)S(1)}, f32[2,128,128]{2,1,0:T(8,128)}, u32[]{:S(2)}) copy-start(f32[2,128,128]{2,1,0:T(8,128)} %inv_hbm.1) | copy-start | bytes 393220
